TPU v7x, 128 devices: a whole 4x4x4 slice. The times are simulated.
128 devices in a mesh: feat: 8 (over x, core), rows: 16 (over z, y).
Axes of the slice: x: 4, y: 4, z: 4, core: 2. Of those that a mesh axis runs over, the one named last changes fastest.
Arguments:
- features: bfloat16 [128, 128, 768], P('feat', None, 'rows'), may hold values from -6 to 6
- w_in: bfloat16 [128, 256], replicated, may hold values from -0.5 to 0.5
- bias: float32 [256], replicated, may hold values from -4 to 4
- tiles: bfloat16 [768, 8, 128, 128], P(('feat', 'rows')), may hold values from 0 to 1, as said below
- tile_cols: int32 [768, 8], P(('feat', 'rows')), may hold values from 0 to 767, as said below
- tile_counts: int32 [768], P(('feat', 'rows')), may hold values from 1 to 8, as said below
- cotangent: bfloat16 [98304, 256], P(('feat', 'rows')), may hold values from -6 to 6
Outputs:
- hidden: bfloat16 [98304, 256], P(('feat', 'rows'))
- weight_grad: float32 [128, 256], P('feat')
Inputs may be any that keep to these rules, and one draw needn't show every extreme that they name: Each block row's count lies between 1 and 8; in every draw some device owns a block row with 8 live slots. Slots k >= tile_counts[I] are ignored. `tile_cols`: block row I on the device owning blocks s * 6 to s * 6 + 6 - 1 (s = I // 6) names column blocks J with J // 96 = I // 96 and (J - (s % 16) * 6 + 2) mod 96 below 10: its own blocks or up to 2 blocks of the neighbouring devices in its cycle, wrapping; both ends are reached. `tiles`: entries are 0 or 1.
All inputs are finite; a program needn't handle non-finite values.
Results may differ from a plain program's by a relative error of at most 0.008.
Values may be sent and summed in bfloat16 or wider, within the bound.
No kernel may reach another device: no remote copies, remote signals or barrier semaphores. Data moves between devices by JAX's collectives and lax.ppermute only.
A program may use at most 64 MiB of HBM per device.

v0:
```python
import jax
import jax.numpy as jnp
from jax import lax
from jax.sharding import PartitionSpec as P

HALO_BLK = 2


def padded(cells, sides, width):
    for axis, dim in sides:
        count = lax.axis_size(axis)
        head = lax.slice_in_dim(cells, 0, width, axis=dim)
        tail = lax.slice_in_dim(cells, cells.shape[dim] - width, cells.shape[dim], axis=dim)
        cells = jnp.concatenate(
            [
                lax.ppermute(tail, axis, [(i, (i + 1) % count) for i in range(count)]),
                cells,
                lax.ppermute(head, axis, [((i + 1) % count, i) for i in range(count)]),
            ],
            axis=dim,
        )
    return cells


def shifted(block, axis, distance):
    devices = range(lax.axis_size(axis))
    route = [((i - distance) % len(devices), i) for i in devices]
    return lax.ppermute(block, axis, route)


def gelu_parts(values):
    inner = 0.7978845608 * (values + 0.044715 * values * values * values)
    tangent = jnp.tanh(inner)
    output = 0.5 * values * (1.0 + tangent)
    slope = 0.5 * (1.0 + tangent) + 0.5 * values * (1.0 - tangent * tangent) * 0.7978845608 * (
        1.0 + 3.0 * 0.044715 * values * values
    )
    return (output, slope)


def halo_projected(projected, margin):
    return padded(projected, (("rows", 0),), margin)


def body(features, w_in, bias, tiles, tile_cols, tile_counts, cotangent):
    block_rows, slot_count, tile_side, unused_side = tiles.shape
    hidden_width = w_in.shape[1]
    feat_size = lax.axis_size("feat")
    row_size = lax.axis_size("rows")
    slice_width = w_in.shape[0] // feat_size
    nodes_dev = block_rows * tile_side
    sub_rows = nodes_dev // row_size
    feat_id = lax.axis_index("feat")
    row_id = lax.axis_index("rows")
    margin = HALO_BLK * tile_side
    w_own = lax.dynamic_slice_in_dim(w_in, feat_id * slice_width, slice_width, 0)
    partial_value = jnp.einsum(
        "cdn,ch->dnh", features, w_own, preferred_element_type=jnp.float32
    ).astype(jnp.bfloat16)
    received = lax.all_to_all(
        partial_value, ("feat", "rows"), split_axis=0, concat_axis=0, tiled=True
    )
    received = received.reshape(feat_size, nodes_dev, hidden_width)
    projected = jnp.sum(received.astype(jnp.float32), axis=0).astype(jnp.bfloat16)
    extended = halo_projected(projected, margin)
    ext_count = block_rows + 2 * HALO_BLK
    ext_blocks = extended.reshape(ext_count, tile_side, hidden_width)
    cycle_size = block_rows * row_size
    local_cols = (tile_cols - feat_id * cycle_size - row_id * block_rows + HALO_BLK) % cycle_size
    slot_ids = jnp.arange(slot_count, dtype=jnp.int32)
    live_slot = (slot_ids[None, :] < tile_counts[:, None]).astype(jnp.bfloat16)
    masked = tiles * live_slot[:, :, None, None]
    degree = jnp.sum(masked, axis=(1, 3), dtype=jnp.float32)
    neighbours = ext_blocks[local_cols]
    summed_rows = jnp.einsum(
        "bkij,bkjh->bih", masked, neighbours, preferred_element_type=jnp.float32
    )
    own_rows = projected.reshape(block_rows, tile_side, hidden_width).astype(jnp.float32)
    pre_act = (own_rows + summed_rows) / (degree[:, :, None] + 1.0) + bias
    activated, slope = gelu_parts(pre_act)
    hidden = activated.astype(jnp.bfloat16).reshape(nodes_dev, hidden_width)
    scaled = (
        cotangent.reshape(block_rows, tile_side, hidden_width).astype(jnp.float32)
        * slope
        / (degree[:, :, None] + 1.0)
    ).astype(jnp.bfloat16)
    targets = jnp.arange(ext_count, dtype=jnp.int32)
    onehot = (local_cols[:, :, None] == targets[None, None, :]).astype(jnp.bfloat16)
    combined = jnp.einsum(
        "bkq,bkij->qbij", onehot, masked, preferred_element_type=jnp.float32
    ).astype(jnp.bfloat16)
    ext_sums = jnp.einsum("qbij,bih->qjh", combined, scaled, preferred_element_type=jnp.float32)
    from_before = shifted(ext_sums[block_rows + HALO_BLK :].astype(jnp.bfloat16), "rows", 1).astype(
        jnp.float32
    )
    from_after = shifted(ext_sums[:HALO_BLK].astype(jnp.bfloat16), "rows", -1).astype(jnp.float32)
    own_sums = ext_sums[HALO_BLK : HALO_BLK + block_rows] + scaled.astype(jnp.float32)
    own_sums = own_sums.at[:HALO_BLK].add(from_before)
    own_sums = own_sums.at[block_rows - HALO_BLK :].add(from_after)
    grad_proj = own_sums.astype(jnp.bfloat16).reshape(nodes_dev, hidden_width)
    pieces = lax.all_to_all(
        grad_proj.reshape(row_size, sub_rows, hidden_width),
        "rows",
        split_axis=0,
        concat_axis=0,
        tiled=True,
    )
    grad_slice = jnp.einsum(
        "cdn,dnh->ch",
        features,
        lax.all_gather(pieces, "feat", axis=0, tiled=True),
        preferred_element_type=jnp.float32,
    )
    weight_grad = lax.psum(grad_slice, "rows")
    return (hidden, weight_grad)


def solution(mesh):
    in_specs = (
        P("feat", None, "rows"),
        P(),
        P(),
        P(("feat", "rows"), None, None, None),
        P(("feat", "rows"), None),
        P(("feat", "rows")),
        P(("feat", "rows"), None),
    )
    out_specs = (P(("feat", "rows"), None), P("feat", None))
    return jax.shard_map(body, mesh=mesh, in_specs=in_specs, out_specs=out_specs, check_vma=False)
```

profile of v0, /device:TPU:0, one launch (start us, length us, event | category | flops | bytes accessed | tf_op | source)
XLA Modules:
  0.0 216.6 jit_solution(2524314712389904341)
XLA Ops:
  7.2 0.8 copy-done
  8.0 1.9 convert_bitcast_fusion.1
  9.9 3.2 %copy.17 = bf16[128,48,256]{2,1,0:T(8,128)(2,1)} copy(bf16[128,48,256]{0,2,1:T(8,128)(2,1)S(1)} %convert_bitcast_fusion.1) | data formatting | bytes 6291456 | tf_op jit(solution)/shard_map/convert_element_type | solution.py:59
  13.1 11.1 %all-to-all-start = ((bf16[128,48,256]{2,1,0:T(8,128)(2,1)}), bf16[128,48,256]{2,1,0:T(8,128)(2,1)S(1)}, u32[]{:S(2)}, u32[]{:S(2)}) async-start(bf16[128,48,256]{2,1,0:T(8,128)(2,1)} %copy.17), calls=%async_computation | async-start | bytes 6291456 | tf_op jit(solution)/shard_map/all_to_all | solution.py:60
  24.4 2.0 convert_reduce_fusion
  26.5 1.1 copy-done.1
  27.6 3.1 %convert_bitcast_fusion = bf16[10,6,128,128]{3,0,2,1:T(8,128)(2,1)} fusion(bf16[6,8,128,128]{3,2,1,0:T(8,128)(2,1)S(1)} %get-tuple-element.27, s32[6,8]{1,0:T(8,128)S(1)} %get-tuple-element.29), kind=kOutput, calls=%fused_computation.2 | convolution fusion | flops 16712160 | bytes 3539136 | tf_op jit(solution)/shard_map/bkq,bkij->qbij/dot_general | solution.py:89
  30.7 33.8 %all-to-all-done = bf16[128,48,256]{2,1,0:T(8,128)(2,1)S(1)} async-done(((bf16[128,48,256]{2,1,0:T(8,128)(2,1)}), bf16[128,48,256]{2,1,0:T(8,128)(2,1)S(1)}, u32[]{:S(2)}, u32[]{:S(2)}) %all-to-all-start) | async-done | bytes 3145760 | tf_op jit(solution)/shard_map/all_to_all | solution.py:60
  65.0 0.7 copy-done.4
  66.4 4.7 %collective-permute-start.1 = (bf16[256,256]{1,0:T(8,128)(2,1)S(1)}, bf16[256,256]{1,0:T(8,128)(2,1)S(1)}, u32[]{:S(2)}, u32[]{:S(2)}) collective-permute-start(bf16[256,256]{1,0:T(8,128)(2,1)S(1)} %get-tuple-element.35), channel_id=1, source_target_pairs={{1,0},{2,1},{3,2},{4,3},{5,4},{6,5},{7,6},{8,7},{9,8},{10,9},{11,1... | collective-permute-start | bytes 393224 | tf_op jit(solution)/shard_map/ppermute | solution.py:18
  71.2 2.9 %collective-permute-done = bf16[256,256]{1,0:T(8,128)(2,1)S(1)} collective-permute-done((bf16[256,256]{1,0:T(8,128)(2,1)S(1)}, bf16[256,256]{1,0:T(8,128)(2,1)S(1)}, u32[]{:S(2)}, u32[]{:S(2)}) %collective-permute-start) | collective-permute-done | bytes 131104 | tf_op jit(solution)/shard_map/ppermute | solution.py:16
  74.1 1.0 pad_maximum_fusion
  75.2 2.5 %gather_fusion = bf16[48,128,256]{2,1,0:T(8,128)(2,1)} fusion(bf16[10,128,256]{2,1,0:T(8,128)(2,1)S(1)} %bitcast.47, s32[1024]{0:T(1024)S(1)} %pad_clamp_fusion), kind=kCustom, calls=%fused_computation | custom fusion | bytes 6291648 | tf_op jit(solution)/shard_map/gather | solution.py:74
  77.7 2.8 %fusion.8 = f32[6,128,256]{2,1,0:T(8,128)S(1)} fusion(bf16[6,8,128,128]{3,2,1,0:T(8,128)(2,1)S(1)} %copy-done.2, bf16[6,8,128,256]{3,2,1,0:T(8,128)(2,1)} %bitcast.49, bf16[6,128,256]{2,1,0:T(8,128)(2,1)S(1)} %bitcast.50, f32[256]{0:T(256)S(1)} %copy-done.10, f32[6,128]{1,0:T(8,128)S(1)} %broadcast_add_fusion), kind=kOutput, calls=%fused_computation.12 | convolution fusion | flops 403439616 | bytes 5902336 | tf_op jit(solution)/shard_map/bkij,bkjh->bih/dot_general | solution.py:75
  80.6 1.5 fusion.32
  82.2 1.4 slice_add_fusion
  83.6 5.3 %collective-permute-start.3 = (bf16[2,128,256]{2,1,0:T(8,128)(2,1)S(1)}, bf16[2,128,256]{2,1,0:T(8,128)(2,1)S(1)}, u32[]{:S(2)}, u32[]{:S(2)}) collective-permute-start(bf16[2,128,256]{2,1,0:T(8,128)(2,1)S(1)} %get-tuple-element.32), channel_id=1, source_target_pairs={{1,0},{2,1},{3,2},{4,3},{5,4},{6,5},{7,6},{8,7},{9,8},{10,9},{11,1... | collective-permute-start | bytes 393224 | tf_op jit(solution)/shard_map/ppermute | solution.py:28
  88.9 1.6 collective-permute-done.2
  90.5 0.9 collective-permute-done.3
  91.5 16.3 %all_to_all.10 = bf16[16,48,256]{2,1,0:T(8,128)(2,1)S(1)} all-to-all(bf16[16,48,256]{2,1,0:T(8,128)(2,1)S(1)} %bitcast.51), channel_id=1, replica_groups=mesh['feat'=8,'rows'=16] {'rows'}, dimensions={0} | all-to-all | bytes 786432 | tf_op jit(solution)/shard_map/all_to_all | solution.py:101
  107.9 0.9 copy.20
  108.8 24.0 %all-gather.2.cloned.1.call-done = bf16[128,48,256]{2,0,1:T(8,128)(2,1)} async-done(((bf16[16,48,256]{2,0,1:T(8,128)(2,1)}), bf16[128,48,256]{2,0,1:T(8,128)(2,1)}) %all-gather.2.cloned.1.call-update) | async-done | bytes 3145744 | tf_op jit(solution)/shard_map/all_gather | solution.py:111
  132.8 2.4 %convolution_bitcast_fusion.1 = f32[16,256]{1,0:T(8,128)S(1)} fusion(bf16[128,48,256]{2,0,1:T(8,128)(2,1)} %all-gather.2.cloned.1.call-done, bf16[16,128,48]{1,2,0:T(8,128)(2,1)S(1)} %copy-done.6), kind=kOutput, calls=%fused_computation.15 | convolution fusion | flops 50331648 | bytes 3358720 | tf_op jit(solution)/shard_map/cdn,dnh->ch/dot_general | solution.py:108
  135.2 74.5 %psum.7 = f32[16,256]{1,0:T(8,128)} all-reduce(f32[16,256]{1,0:T(8,128)S(1)} %convolution_bitcast_fusion.1), channel_id=1, replica_groups=mesh['feat'=8,'rows'=16] {'rows'}, use_global_device_ids=true, to_apply=%region_2.3 | all-reduce | flops 4096 | bytes 32768 | tf_op jit(solution)/shard_map/psum | solution.py:114
  (35 shorter events, 1.7 us)
Async XLA Ops:
  7.2 0.8 copy-start
  13.1 11.2 %copy-start.9 = (s32[6]{0:T(128)S(1)}, s32[6]{0:T(128)}, u32[]{:S(2)}) copy-start(s32[6]{0:T(128)} %param.16) | copy-start | bytes 76
  13.1 11.3 %copy-start.8 = (s32[6,8]{1,0:T(8,128)S(1)}, s32[6,8]{1,0:T(8,128)}, u32[]{:S(2)}) copy-start(s32[6,8]{1,0:T(8,128)} %param.15) | copy-start | bytes 580
  13.1 51.4 %all-to-all-start = ((bf16[128,48,256]{2,1,0:T(8,128)(2,1)}), bf16[128,48,256]{2,1,0:T(8,128)(2,1)S(1)}, u32[]{:S(2)}, u32[]{:S(2)}) async-start(bf16[128,48,256]{2,1,0:T(8,128)(2,1)} %copy.17), calls=%async_computation | async-start | bytes 6291456 | tf_op jit(solution)/shard_map/all_to_all | solution.py:60
  24.3 108.5 %all-gather.2.cloned.1.call-start = ((), (), s32[]{:S(2)}) async-start(), calls=%async_computation.2 | async-start | bytes 3538944 | tf_op jit(solution)/shard_map/all_gather | solution.py:111
  26.5 1.1 copy-start.1
  64.9 0.7 copy-start.4
  65.7 8.4 %collective-permute-start = (bf16[256,256]{1,0:T(8,128)(2,1)S(1)}, bf16[256,256]{1,0:T(8,128)(2,1)S(1)}, u32[]{:S(2)}, u32[]{:S(2)}) collective-permute-start(bf16[256,256]{1,0:T(8,128)(2,1)S(1)} %get-tuple-element.34), channel_id=1, source_target_pairs={{0,1},{1,2},{2,3},{3,4},{4,5},{5,6},{6,7},{7,8},{8,9},{9,10},{10,1... | collective-permute-start | bytes 393224 | tf_op jit(solution)/shard_map/ppermute | solution.py:16
  66.4 7.7 %collective-permute-start.1 = (bf16[256,256]{1,0:T(8,128)(2,1)S(1)}, bf16[256,256]{1,0:T(8,128)(2,1)S(1)}, u32[]{:S(2)}, u32[]{:S(2)}) collective-permute-start(bf16[256,256]{1,0:T(8,128)(2,1)S(1)} %get-tuple-element.35), channel_id=1, source_target_pairs={{1,0},{2,1},{3,2},{4,3},{5,4},{6,5},{7,6},{8,7},{9,8},{10,9},{11,1... | collective-permute-start | bytes 393224 | tf_op jit(solution)/shard_map/ppermute | solution.py:18
  75.1 2.6 %copy-start.2 = (bf16[6,8,128,128]{3,2,1,0:T(8,128)(2,1)S(1)}, bf16[6,8,128,128]{3,2,1,0:T(8,128)(2,1)}, u32[]{:S(2)}) copy-start(bf16[6,8,128,128]{3,2,1,0:T(8,128)(2,1)} %copy-done.1) | copy-start | bytes 4718596
  75.1 2.6 %copy-start.5 = (bf16[768,256]{1,0:T(8,128)(2,1)S(1)}, bf16[768,256]{1,0:T(8,128)(2,1)}, u32[]{:S(2)}) copy-start(bf16[768,256]{1,0:T(8,128)(2,1)} %copy-done.4) | copy-start | bytes 1179652
  75.1 2.6 %copy-start.10 = (f32[256]{0:T(256)S(1)}, f32[256]{0:T(256)}, u32[]{:S(2)}) copy-start(f32[256]{0:T(256)} %param.13) | copy-start | bytes 3076
  77.7 2.8 %copy-start.3 = (bf16[10,6,128,128]{3,0,2,1:T(8,128)(2,1)S(1)}, bf16[10,6,128,128]{3,0,2,1:T(8,128)(2,1)}, u32[]{:S(2)}) copy-start(bf16[10,6,128,128]{3,0,2,1:T(8,128)(2,1)} %convert_bitcast_fusion) | copy-start | bytes 5898244
  77.7 2.9 %copy-start.7 = (bf16[768,256]{1,0:T(8,128)(2,1)S(1)}, bf16[768,256]{1,0:T(8,128)(2,1)}, u32[]{:S(2)}) copy-start(bf16[768,256]{1,0:T(8,128)(2,1)} %param.17) | copy-start | bytes 1179652
  82.1 8.4 %collective-permute-start.2 = (bf16[2,128,256]{2,1,0:T(8,128)(2,1)S(1)}, bf16[2,128,256]{2,1,0:T(8,128)(2,1)S(1)}, u32[]{:S(2)}, u32[]{:S(2)}) collective-permute-start(bf16[2,128,256]{2,1,0:T(8,128)(2,1)S(1)} %get-tuple-element.33), channel_id=1, source_target_pairs={{15,0},{0,1},{1,2},{2,3},{3,4},{4,5},{5,6},{6,7},{7,8},{8,9},{9,10... | collective-permute-start | bytes 393224 | tf_op jit(solution)/shard_map/ppermute | solution.py:28
  82.2 50.6 %copy-start.6 = (bf16[16,128,48]{1,2,0:T(8,128)(2,1)S(1)}, bf16[16,128,48]{1,2,0:T(8,128)(2,1)}, u32[]{:S(2)}) copy-start(bf16[16,128,48]{1,2,0:T(8,128)(2,1)} %param.11) | copy-start | bytes 589828
  83.6 7.9 %collective-permute-start.3 = (bf16[2,128,256]{2,1,0:T(8,128)(2,1)S(1)}, bf16[2,128,256]{2,1,0:T(8,128)(2,1)S(1)}, u32[]{:S(2)}, u32[]{:S(2)}) collective-permute-start(bf16[2,128,256]{2,1,0:T(8,128)(2,1)S(1)} %get-tuple-element.32), channel_id=1, source_target_pairs={{1,0},{2,1},{3,2},{4,3},{5,4},{6,5},{7,6},{8,7},{9,8},{10,9},{11,1... | collective-permute-start | bytes 393224 | tf_op jit(solution)/shard_map/ppermute | solution.py:28
Sparse Core Ops, SparseCore 0:
  108.9 23.8 all-gather.1
where the time goes:
time: 217 us
  blocking collectives  90.9 us (42%)
  waiting for transfers between devices  63.2 us (29%)
  starting transfers between devices  22 us (10%)
  between operations  14.2 us (7%)
  matrix products  11.6 us (5%)
  local copies, waits for them, and re-layouts  9.55 us (4%)
  other arithmetic  5.11 us (2%)
    psum x1, blocking collectives, body(): weight_grad = lax.psum(grad_slice, 'rows')  74.5 us
    all_to_all x1, waiting for transfers between devices, body(): lax.all_to_all(partial_value, ('feat', 'rows'), split_axis=0, concat_axis...  33.8 us
    all_gather x1, waiting for transfers between devices, body(): lax.all_gather(pieces, 'feat', axis=0, tiled=True)  24 us
    all_to_all x1, blocking collectives, body(): lax.all_to_all(grad_proj.reshape(row_size, sub_rows, hidden_width), 'rows...  16.3 us
    all_to_all x1, starting transfers between devices, body(): lax.all_to_all(partial_value, ('feat', 'rows'), split_axis=0, concat_axis...  11.1 us
    ppermute x2, starting transfers between devices, shifted(): return lax.ppermute(block, axis, route)  5.42 us
    ppermute x1, starting transfers between devices, padded(): lax.ppermute(head, axis, [((i + 1) % count, i) for i in range(count)])  4.74 us
  transfers between devices with their start and end apart: 6, of which 5 were waited for; matrix products, arithmetic and copies ran while one was open for 3% of the time, Pallas kernels for 0%

commit v1 on v0

--- a/solution.py
+++ b/solution.py
@@ -111,7 +111,7 @@
         lax.all_gather(pieces, "feat", axis=0, tiled=True),
         preferred_element_type=jnp.float32,
     )
-    weight_grad = lax.psum(grad_slice, "rows")
+    weight_grad = jnp.sum(lax.all_gather(grad_slice, "rows"), axis=0)
     return (hidden, weight_grad)
 
 

time: 217 us -> 167 us (0.77)
  blocking collectives: 90.9 us -> 40.3 us
    psum x1 -> x0, blocking collectives: 74.5 us -> none  [body(): weight_grad = lax.psum(grad_slice, 'rows')]
    all_gather x0 -> x1, blocking collectives: none -> 24 us  [body(): weight_grad = jnp.sum(lax.all_gather(grad_slice, 'rows'), axis=0)]
  transfers between devices with their start and end apart: 6 -> 6, of which waited for: 5 -> 5; matrix products, arithmetic and copies ran while one was open for 3% -> 4% of each run, Pallas kernels for 0% -> 0%
where the time goes in v1:
time: 167 us
  waiting for transfers between devices  63.2 us (38%)
  blocking collectives  40.3 us (24%)
  starting transfers between devices  22 us (13%)
  between operations  14.2 us (9%)
  matrix products  11.6 us (7%)
  local copies, waits for them, and re-layouts  9.55 us (6%)
  other arithmetic  5.74 us (3%)
    all_to_all x1, waiting for transfers between devices, body(): lax.all_to_all(partial_value, ('feat', 'rows'), split_axis=0, concat_axis...  33.8 us
    all_gather x1, waiting for transfers between devices, body(): lax.all_gather(pieces, 'feat', axis=0, tiled=True)  24 us
    all_gather x1, blocking collectives, body(): weight_grad = jnp.sum(lax.all_gather(grad_slice, 'rows'), axis=0)  24 us
    all_to_all x1, blocking collectives, body(): lax.all_to_all(grad_proj.reshape(row_size, sub_rows, hidden_width), 'rows...  16.3 us
    all_to_all x1, starting transfers between devices, body(): lax.all_to_all(partial_value, ('feat', 'rows'), split_axis=0, concat_axis...  11.1 us
    ppermute x2, starting transfers between devices, shifted(): return lax.ppermute(block, axis, route)  5.42 us
    ppermute x1, starting transfers between devices, padded(): lax.ppermute(head, axis, [((i + 1) % count, i) for i in range(count)])  4.74 us
  transfers between devices with their start and end apart: 6, of which 5 were waited for; matrix products, arithmetic and copies ran while one was open for 4% of the time, Pallas kernels for 0%

profile of v1, /device:TPU:0, one launch (start us, length us, event | category | flops | bytes accessed | tf_op | source)
XLA Modules:
  0.0 166.6 jit_solution(13654095066257501739)
XLA Ops:
  7.2 0.8 copy-done
  8.0 1.9 %convert_bitcast_fusion.1 = bf16[128,48,256]{0,2,1:T(8,128)(2,1)S(1)} fusion(bf16[16,128,48]{1,2,0:T(8,128)(2,1)} %param.11, bf16[128,256]{1,0:T(8,128)(2,1)S(1)} %copy-done, s32[]{:T(128)S(6)} %select_n.13), kind=kOutput, calls=%fused_computation.4 | convolution fusion | flops 51904512 | bytes 3350532 | tf_op jit(solution)/shard_map/cdn,ch->dnh/dot_general | solution.py:57
  9.9 3.2 %copy.17 = bf16[128,48,256]{2,1,0:T(8,128)(2,1)} copy(bf16[128,48,256]{0,2,1:T(8,128)(2,1)S(1)} %convert_bitcast_fusion.1) | data formatting | bytes 6291456 | tf_op jit(solution)/shard_map/convert_element_type | solution.py:59
  13.1 11.1 %all-to-all-start = ((bf16[128,48,256]{2,1,0:T(8,128)(2,1)}), bf16[128,48,256]{2,1,0:T(8,128)(2,1)S(1)}, u32[]{:S(2)}, u32[]{:S(2)}) async-start(bf16[128,48,256]{2,1,0:T(8,128)(2,1)} %copy.17), calls=%async_computation | async-start | bytes 6291456 | tf_op jit(solution)/shard_map/all_to_all | solution.py:60
  24.4 2.0 %convert_reduce_fusion = (f32[6,128]{1,0:T(8,128)S(1)}, bf16[6,8,128,128]{3,2,1,0:T(8,128)(2,1)S(1)}) fusion(bf16[6,8,128,128]{3,2,1,0:T(8,128)(2,1)} %param.14, bf16[6,8]{1,0:T(8,128)(2,1)S(1)} %fusion.27), kind=kLoop, calls=%fused_computation.3 | loop fusion | flops 2358528 | bytes 3148896 | tf_op jit(solution)/shard_map/reduce_sum | solution.py:73
  26.5 1.1 copy-done.1
  27.6 3.1 %convert_bitcast_fusion = bf16[10,6,128,128]{3,0,2,1:T(8,128)(2,1)} fusion(bf16[6,8,128,128]{3,2,1,0:T(8,128)(2,1)S(1)} %get-tuple-element.27, s32[6,8]{1,0:T(8,128)S(1)} %get-tuple-element.29), kind=kOutput, calls=%fused_computation.2 | convolution fusion | flops 16712160 | bytes 3539136 | tf_op jit(solution)/shard_map/bkq,bkij->qbij/dot_general | solution.py:89
  30.7 33.8 %all-to-all-done = bf16[128,48,256]{2,1,0:T(8,128)(2,1)S(1)} async-done(((bf16[128,48,256]{2,1,0:T(8,128)(2,1)}), bf16[128,48,256]{2,1,0:T(8,128)(2,1)S(1)}, u32[]{:S(2)}, u32[]{:S(2)}) %all-to-all-start) | async-done | bytes 3145760 | tf_op jit(solution)/shard_map/all_to_all | solution.py:60
  65.0 0.7 copy-done.4
  66.4 4.7 %collective-permute-start.1 = (bf16[256,256]{1,0:T(8,128)(2,1)S(1)}, bf16[256,256]{1,0:T(8,128)(2,1)S(1)}, u32[]{:S(2)}, u32[]{:S(2)}) collective-permute-start(bf16[256,256]{1,0:T(8,128)(2,1)S(1)} %get-tuple-element.35), channel_id=1, source_target_pairs={{1,0},{2,1},{3,2},{4,3},{5,4},{6,5},{7,6},{8,7},{9,8},{10,9},{11,1... | collective-permute-start | bytes 393224 | tf_op jit(solution)/shard_map/ppermute | solution.py:18
  71.2 2.9 %collective-permute-done = bf16[256,256]{1,0:T(8,128)(2,1)S(1)} collective-permute-done((bf16[256,256]{1,0:T(8,128)(2,1)S(1)}, bf16[256,256]{1,0:T(8,128)(2,1)S(1)}, u32[]{:S(2)}, u32[]{:S(2)}) %collective-permute-start) | collective-permute-done | bytes 131104 | tf_op jit(solution)/shard_map/ppermute | solution.py:16
  74.1 1.0 pad_maximum_fusion
  75.2 2.5 %gather_fusion = bf16[48,128,256]{2,1,0:T(8,128)(2,1)} fusion(bf16[10,128,256]{2,1,0:T(8,128)(2,1)S(1)} %bitcast.48, s32[1024]{0:T(1024)S(1)} %pad_clamp_fusion), kind=kCustom, calls=%fused_computation | custom fusion | bytes 6291648 | tf_op jit(solution)/shard_map/gather | solution.py:74
  77.7 2.8 %fusion.8 = f32[6,128,256]{2,1,0:T(8,128)S(1)} fusion(bf16[6,8,128,128]{3,2,1,0:T(8,128)(2,1)S(1)} %copy-done.2, bf16[6,8,128,256]{3,2,1,0:T(8,128)(2,1)} %bitcast.50, bf16[6,128,256]{2,1,0:T(8,128)(2,1)S(1)} %bitcast.51, f32[256]{0:T(256)S(1)} %copy-done.10, f32[6,128]{1,0:T(8,128)S(1)} %broadcast_add_fusion), kind=kOutput, calls=%fused_computation.12 | convolution fusion | flops 403439616 | bytes 5902336 | tf_op jit(solution)/shard_map/bkij,bkjh->bih/dot_general | solution.py:75
  80.6 1.5 fusion.32
  82.2 1.4 slice_add_fusion
  83.6 5.3 %collective-permute-start.3 = (bf16[2,128,256]{2,1,0:T(8,128)(2,1)S(1)}, bf16[2,128,256]{2,1,0:T(8,128)(2,1)S(1)}, u32[]{:S(2)}, u32[]{:S(2)}) collective-permute-start(bf16[2,128,256]{2,1,0:T(8,128)(2,1)S(1)} %get-tuple-element.32), channel_id=1, source_target_pairs={{1,0},{2,1},{3,2},{4,3},{5,4},{6,5},{7,6},{8,7},{9,8},{10,9},{11,1... | collective-permute-start | bytes 393224 | tf_op jit(solution)/shard_map/ppermute | solution.py:28
  88.9 1.6 collective-permute-done.2
  90.5 0.9 collective-permute-done.3
  91.5 16.3 %all_to_all.10 = bf16[16,48,256]{2,1,0:T(8,128)(2,1)S(1)} all-to-all(bf16[16,48,256]{2,1,0:T(8,128)(2,1)S(1)} %bitcast.52), channel_id=1, replica_groups=mesh['feat'=8,'rows'=16] {'rows'}, dimensions={0} | all-to-all | bytes 786432 | tf_op jit(solution)/shard_map/all_to_all | solution.py:101
  107.9 0.9 copy.20
  108.8 24.0 %all-gather.3.cloned.1.call-done = bf16[128,48,256]{2,0,1:T(8,128)(2,1)} async-done(((bf16[16,48,256]{2,0,1:T(8,128)(2,1)}), bf16[128,48,256]{2,0,1:T(8,128)(2,1)}) %all-gather.3.cloned.1.call-update) | async-done | bytes 3145744 | tf_op jit(solution)/shard_map/all_gather | solution.py:111
  132.8 2.4 %convolution_bitcast_fusion.1 = f32[16,256]{1,0:T(8,128)S(1)} fusion(bf16[128,48,256]{2,0,1:T(8,128)(2,1)} %all-gather.3.cloned.1.call-done, bf16[16,128,48]{1,2,0:T(8,128)(2,1)S(1)} %copy-done.6), kind=kOutput, calls=%fused_computation.15 | convolution fusion | flops 50331648 | bytes 3358720 | tf_op jit(solution)/shard_map/cdn,dnh->ch/dot_general | solution.py:108
  135.2 24.0 %all-gather = f32[256,256]{1,0:T(8,128)S(1)} all-gather(f32[16,256]{1,0:T(8,128)S(1)} %convolution_bitcast_fusion.1), channel_id=2, replica_groups=mesh['feat'=8,'rows'=16] {'rows'}, dimensions={0}, use_global_device_ids=true | all-gather | bytes 278528 | tf_op jit(solution)/shard_map/all_gather | solution.py:114
  (36 shorter events, 2.4 us)
Async XLA Ops:
  7.2 0.8 copy-start
  13.1 11.2 %copy-start.9 = (s32[6]{0:T(128)S(1)}, s32[6]{0:T(128)}, u32[]{:S(2)}) copy-start(s32[6]{0:T(128)} %param.16) | copy-start | bytes 76
  13.1 11.3 %copy-start.8 = (s32[6,8]{1,0:T(8,128)S(1)}, s32[6,8]{1,0:T(8,128)}, u32[]{:S(2)}) copy-start(s32[6,8]{1,0:T(8,128)} %param.15) | copy-start | bytes 580
  13.1 51.4 %all-to-all-start = ((bf16[128,48,256]{2,1,0:T(8,128)(2,1)}), bf16[128,48,256]{2,1,0:T(8,128)(2,1)S(1)}, u32[]{:S(2)}, u32[]{:S(2)}) async-start(bf16[128,48,256]{2,1,0:T(8,128)(2,1)} %copy.17), calls=%async_computation | async-start | bytes 6291456 | tf_op jit(solution)/shard_map/all_to_all | solution.py:60
  24.3 108.5 %all-gather.3.cloned.1.call-start = ((), (), s32[]{:S(2)}) async-start(), calls=%async_computation.2 | async-start | bytes 3538944 | tf_op jit(solution)/shard_map/all_gather | solution.py:111
  26.5 1.1 copy-start.1
  64.9 0.7 copy-start.4
  65.7 8.4 %collective-permute-start = (bf16[256,256]{1,0:T(8,128)(2,1)S(1)}, bf16[256,256]{1,0:T(8,128)(2,1)S(1)}, u32[]{:S(2)}, u32[]{:S(2)}) collective-permute-start(bf16[256,256]{1,0:T(8,128)(2,1)S(1)} %get-tuple-element.34), channel_id=1, source_target_pairs={{0,1},{1,2},{2,3},{3,4},{4,5},{5,6},{6,7},{7,8},{8,9},{9,10},{10,1... | collective-permute-start | bytes 393224 | tf_op jit(solution)/shard_map/ppermute | solution.py:16
  66.4 7.7 %collective-permute-start.1 = (bf16[256,256]{1,0:T(8,128)(2,1)S(1)}, bf16[256,256]{1,0:T(8,128)(2,1)S(1)}, u32[]{:S(2)}, u32[]{:S(2)}) collective-permute-start(bf16[256,256]{1,0:T(8,128)(2,1)S(1)} %get-tuple-element.35), channel_id=1, source_target_pairs={{1,0},{2,1},{3,2},{4,3},{5,4},{6,5},{7,6},{8,7},{9,8},{10,9},{11,1... | collective-permute-start | bytes 393224 | tf_op jit(solution)/shard_map/ppermute | solution.py:18
  75.1 2.6 %copy-start.2 = (bf16[6,8,128,128]{3,2,1,0:T(8,128)(2,1)S(1)}, bf16[6,8,128,128]{3,2,1,0:T(8,128)(2,1)}, u32[]{:S(2)}) copy-start(bf16[6,8,128,128]{3,2,1,0:T(8,128)(2,1)} %copy-done.1) | copy-start | bytes 4718596
  75.1 2.6 %copy-start.5 = (bf16[768,256]{1,0:T(8,128)(2,1)S(1)}, bf16[768,256]{1,0:T(8,128)(2,1)}, u32[]{:S(2)}) copy-start(bf16[768,256]{1,0:T(8,128)(2,1)} %copy-done.4) | copy-start | bytes 1179652
  75.1 2.6 %copy-start.10 = (f32[256]{0:T(256)S(1)}, f32[256]{0:T(256)}, u32[]{:S(2)}) copy-start(f32[256]{0:T(256)} %param.13) | copy-start | bytes 3076
  77.7 2.8 %copy-start.3 = (bf16[10,6,128,128]{3,0,2,1:T(8,128)(2,1)S(1)}, bf16[10,6,128,128]{3,0,2,1:T(8,128)(2,1)}, u32[]{:S(2)}) copy-start(bf16[10,6,128,128]{3,0,2,1:T(8,128)(2,1)} %convert_bitcast_fusion) | copy-start | bytes 5898244
  77.7 2.9 %copy-start.7 = (bf16[768,256]{1,0:T(8,128)(2,1)S(1)}, bf16[768,256]{1,0:T(8,128)(2,1)}, u32[]{:S(2)}) copy-start(bf16[768,256]{1,0:T(8,128)(2,1)} %param.17) | copy-start | bytes 1179652
  82.1 8.4 %collective-permute-start.2 = (bf16[2,128,256]{2,1,0:T(8,128)(2,1)S(1)}, bf16[2,128,256]{2,1,0:T(8,128)(2,1)S(1)}, u32[]{:S(2)}, u32[]{:S(2)}) collective-permute-start(bf16[2,128,256]{2,1,0:T(8,128)(2,1)S(1)} %get-tuple-element.33), channel_id=1, source_target_pairs={{15,0},{0,1},{1,2},{2,3},{3,4},{4,5},{5,6},{6,7},{7,8},{8,9},{9,10... | collective-permute-start | bytes 393224 | tf_op jit(solution)/shard_map/ppermute | solution.py:28
  82.2 50.6 %copy-start.6 = (bf16[16,128,48]{1,2,0:T(8,128)(2,1)S(1)}, bf16[16,128,48]{1,2,0:T(8,128)(2,1)}, u32[]{:S(2)}) copy-start(bf16[16,128,48]{1,2,0:T(8,128)(2,1)} %param.11) | copy-start | bytes 589828
  83.6 7.9 %collective-permute-start.3 = (bf16[2,128,256]{2,1,0:T(8,128)(2,1)S(1)}, bf16[2,128,256]{2,1,0:T(8,128)(2,1)S(1)}, u32[]{:S(2)}, u32[]{:S(2)}) collective-permute-start(bf16[2,128,256]{2,1,0:T(8,128)(2,1)S(1)} %get-tuple-element.32), channel_id=1, source_target_pairs={{1,0},{2,1},{3,2},{4,3},{5,4},{6,5},{7,6},{8,7},{9,8},{10,9},{11,1... | collective-permute-start | bytes 393224 | tf_op jit(solution)/shard_map/ppermute | solution.py:28
Sparse Core Ops, SparseCore 0:
  108.9 23.8 all-gather.2
